TPU v7x, 256 devices: a whole 4x4x8 slice. The times are simulated.
256 devices in a mesh: blk: 32 (over z_hi, y, core), slab: 8 (over x, z_lo).
Axes of the slice: x: 4, y: 4, z: 8 (z_hi: 4, z_lo: 2; z = z_hi * 2 + z_lo), core: 2. Of those that a mesh axis runs over, the one named last changes fastest.
Arguments:
- interactions: bfloat16 [7040, 65536], P('slab', 'blk'), may hold values from -6 to 6
- user_weight: float32 [7040], P('slab'), may hold values from 0.25 to 4
Outputs:
- gram_tiles: float32 [2, 65536, 2048], P(None, ('blk', 'slab'))
All inputs are finite; a program needn't handle non-finite values.
Results may differ from a plain program's by a relative error of at most 0.015.
Values may be sent and summed in bfloat16 or wider, within the bound.
A program may use at most 128 MiB of HBM per device.

v0:
```python
import jax
import jax.numpy as jnp
from jax import lax
from jax.sharding import PartitionSpec as P

ROUNDS = 2


def passed_along(value, axis, steps):
    count = lax.axis_size(axis)
    pairs = [(source, (source + steps) % count) for source in range(count)]
    return lax.ppermute(value, axis, pairs)


def on_device(interactions, user_weight):
    slabs = lax.axis_size("slab")
    users = interactions.shape[0] * slabs
    scale = 1.0 / jnp.sqrt(jnp.float32(users))
    weighted = (interactions.astype(jnp.float32) * user_weight[:, None] * scale).astype(
        jnp.bfloat16
    )
    partners = []
    moving = interactions
    for step in range(ROUNDS):
        moving = passed_along(moving, "blk", -1)
        partners.append(moving)
    results = []
    for step in range(ROUNDS):
        partner = partners[step]
        results.append(
            lax.psum_scatter(
                lax.dot_general(
                    weighted, partner, (((0,), (0,)), ((), ())), preferred_element_type=jnp.float32
                ).astype(jnp.bfloat16),
                "slab",
                scatter_dimension=0,
                tiled=True,
            ).astype(jnp.float32)
        )
    return jnp.stack(results)


def solution(mesh):
    in_specs = (P("slab", "blk"), P("slab"))
    out_specs = P(None, ("blk", "slab"), None)
    return jax.shard_map(
        on_device, mesh=mesh, in_specs=in_specs, out_specs=out_specs, check_vma=False
    )
```

profile of v0, /device:TPU:1, one launch (start us, length us, event | category | flops | bytes accessed | tf_op | source)
XLA Modules:
  0.0 531.9 jit_solution(11568187129976099117)
XLA Ops:
  6.5 0.0 reduce-scatter.3.cloned.1.call-start
  6.5 3.2 collective-permute-start
  9.8 39.5 %collective-permute-done = bf16[880,2048]{1,0:T(8,128)(2,1)S(1)} collective-permute-done((bf16[880,2048]{1,0:T(8,128)(2,1)}, bf16[880,2048]{1,0:T(8,128)(2,1)S(1)}, u32[]{:S(2)}, u32[]{:S(2)}) %collective-permute-start) | collective-permute-done | bytes 3604512 | tf_op jit(solution)/shard_map/ppermute | solution.py:12
  49.3 0.0 copy-start
  49.3 1.8 copy-done
  51.1 13.6 %convolution_convert_fusion.1 = bf16[2048,2048]{1,0:T(8,128)(2,1)} fusion(bf16[880,2048]{1,0:T(8,128)(2,1)S(1)} %collective-permute-done, bf16[880,2048]{1,0:T(8,128)(2,1)} %param.2, f32[880]{0:T(1024)} %param.3), kind=kOutput, calls=%fused_computation.1 | convolution fusion | flops 7393378304 | bytes 15601088 | tf_op jit(solution)/shard_map/dot_general | solution.py:32
  64.8 0.0 copy-start.1
  64.8 0.0 reduce-scatter.3.cloned.1.call-update
  64.8 0.0 reduce-scatter.5.cloned.1.call-start
  64.8 45.7 %collective-permute-start.1 = (bf16[880,2048]{1,0:T(8,128)(2,1)}, bf16[880,2048]{1,0:T(8,128)(2,1)S(1)}, u32[]{:S(2)}, u32[]{:S(2)}) collective-permute-start(bf16[880,2048]{1,0:T(8,128)(2,1)} %copy-done), channel_id=1, source_target_pairs={{0,248},{8,0},{16,8},{24,16},{32,24},{40,32},{48,40},{56,48},{64,5... | collective-permute-start | bytes 10813448 | tf_op jit(solution)/shard_map/ppermute | solution.py:12
  110.5 6.2 %collective-permute-done.1 = bf16[880,2048]{1,0:T(8,128)(2,1)S(1)} collective-permute-done((bf16[880,2048]{1,0:T(8,128)(2,1)}, bf16[880,2048]{1,0:T(8,128)(2,1)S(1)}, u32[]{:S(2)}, u32[]{:S(2)}) %collective-permute-start.1) | collective-permute-done | bytes 3604512 | tf_op jit(solution)/shard_map/ppermute | solution.py:12
  116.7 0.0 copy-done.1
  116.7 13.7 %convolution_convert_fusion = bf16[2048,2048]{1,0:T(8,128)(2,1)} fusion(bf16[880,2048]{1,0:T(8,128)(2,1)S(1)} %collective-permute-done.1, bf16[880,2048]{1,0:T(8,128)(2,1)} %param.2, f32[880]{0:T(1024)S(1)} %copy-done.1), kind=kOutput, calls=%fused_computation | convolution fusion | flops 7393378304 | bytes 15601088 | tf_op jit(solution)/shard_map/dot_general | solution.py:32
  130.4 0.0 reduce-scatter.5.cloned.1.call-update
  130.4 222.6 %reduce-scatter.3.cloned.1.call-done = bf16[256,2048]{1,0:T(8,128)(2,1)} async-done(((bf16[2048,2048]{1,0:T(8,128)(2,1)}), bf16[256,2048]{1,0:T(8,128)(2,1)}) %reduce-scatter.3.cloned.1.call-update) | async-done | bytes 1048592 | tf_op jit(solution)/shard_map/reduce_scatter | solution.py:31
  353.0 168.2 %reduce-scatter.5.cloned.1.call-done = bf16[256,2048]{1,0:T(8,128)(2,1)} async-done(((bf16[2048,2048]{1,0:T(8,128)(2,1)}), bf16[256,2048]{1,0:T(8,128)(2,1)}) %reduce-scatter.5.cloned.1.call-update) | async-done | bytes 1048592 | tf_op jit(solution)/shard_map/reduce_scatter | solution.py:31
  521.2 3.8 maximum_convert_fusion
Async XLA Ops:
  6.5 346.5 %reduce-scatter.3.cloned.1.call-start = ((), (), s32[]{:S(2)}) async-start(), calls=%async_computation.2 | async-start | bytes 9437184 | tf_op jit(solution)/shard_map/reduce_scatter | solution.py:31
  6.5 42.8 %collective-permute-start = (bf16[880,2048]{1,0:T(8,128)(2,1)}, bf16[880,2048]{1,0:T(8,128)(2,1)S(1)}, u32[]{:S(2)}, u32[]{:S(2)}) collective-permute-start(bf16[880,2048]{1,0:T(8,128)(2,1)} %param.2), channel_id=1, source_target_pairs={{0,248},{8,0},{16,8},{24,16},{32,24},{40,32},{48,40},{56,48},{64,5... | collective-permute-start | bytes 10813448 | tf_op jit(solution)/shard_map/ppermute | solution.py:12
  49.3 1.8 copy-start
  64.8 51.9 %copy-start.1 = (f32[880]{0:T(1024)S(1)}, f32[880]{0:T(1024)}, u32[]{:S(2)}) copy-start(f32[880]{0:T(1024)} %param.3) | copy-start | bytes 10564
  64.8 456.4 %reduce-scatter.5.cloned.1.call-start = ((), (), s32[]{:S(2)}) async-start(), calls=%async_computation.3 | async-start | bytes 9437184 | tf_op jit(solution)/shard_map/reduce_scatter | solution.py:31
  64.8 51.9 %collective-permute-start.1 = (bf16[880,2048]{1,0:T(8,128)(2,1)}, bf16[880,2048]{1,0:T(8,128)(2,1)S(1)}, u32[]{:S(2)}, u32[]{:S(2)}) collective-permute-start(bf16[880,2048]{1,0:T(8,128)(2,1)} %copy-done), channel_id=1, source_target_pairs={{0,248},{8,0},{16,8},{24,16},{32,24},{40,32},{48,40},{56,48},{64,5... | collective-permute-start | bytes 10813448 | tf_op jit(solution)/shard_map/ppermute | solution.py:12
Sparse Core Ops, SparseCore 0:
  64.9 288.0 reduce-scatter.2
  355.6 165.5 reduce-scatter.4
where the time goes:
time: 532 us
  waiting for transfers between devices  437 us (82%)
  starting transfers between devices  49 us (9%)
  matrix products  27.3 us (5%)
  between operations  13.4 us (3%)
    reduce_scatter x2, waiting for transfers between devices, on_device(): lax.psum_scatter(lax.dot_general(weighted, partner, (((0,), (0,)), ((), (...  391 us
    ppermute x2, starting transfers between devices, passed_along(): return lax.ppermute(value, axis, pairs)  48.9 us
    ppermute x2, waiting for transfers between devices, passed_along(): return lax.ppermute(value, axis, pairs)  45.7 us
    dot_general x2, matrix products, on_device(): lax.dot_general(weighted, partner, (((0,), (0,)), ((), ())), preferred_el...  27.3 us
  transfers between devices with their start and end apart: 4, of which 4 were waited for; matrix products, arithmetic and copies ran while one was open for 3% of the time, Pallas kernels for 0%

commit v1 on v0

v1 whole, which is shorter than its diff:
```python
import functools

import jax
import jax.numpy as jnp
from jax import lax
from jax.experimental import pallas as pl
from jax.experimental.pallas import tpu as pltpu
from jax.sharding import PartitionSpec as P

ROUNDS = 2
CHUNKS = 4
RING = 4
PADDED = 896
RELAYED = (1, 3)
MESH = pl.DeviceIdType.MESH


def kernel(
    x_ref,
    weight_ref,
    out_ref,
    own,
    weighted,
    partner,
    relay,
    first_out,
    first_in,
    second_out,
    second_in,
    pair_out,
    pair_in,
    total,
    load_sem,
    block_send,
    block_recv,
    relay_recv,
    first_send,
    first_recv,
    second_send,
    second_recv,
    pair_send,
    pair_recv,
    store_sem,
):
    blk, slab = lax.axis_index("blk"), lax.axis_index("slab")
    blocks = lax.axis_size("blk")
    core, y = lax.rem(blk, 2), lax.rem(blk // 2, 4)
    x, z_lo = slab // 2, lax.rem(slab, 2)
    users = x_ref.shape[0]
    width = x_ref.shape[1] // CHUNKS
    rows = x_ref.shape[1] // RING
    half = rows // 2
    units = ROUNDS * CHUNKS
    seconds = core == 1

    right = (blk, lax.rem(x + 1, RING) * 2 + z_lo)
    left = (blk, lax.rem(x + RING - 1, RING) * 2 + z_lo)
    mate = (blk, x * 2 + 1 - z_lo)
    twin = (blk + 1 - 2 * core, slab)
    back = lax.rem(blk + blocks - 2 - core, blocks) + 1
    before = (back, slab)
    front = lax.rem(blk - core + 2, blocks)
    after = ((front, slab), (front + 1, slab))
    relay_at = (blk - core + 7, slab)
    relay_from = ((blk - core - 6, slab), (blk - core - 5, slab))
    relay_to = (lax.rem(blk - core + blocks - 8, blocks) + 1, slab)
    relay_after = (lax.rem(blk - core + 8, blocks) + 1, slab)

    loads = [
        pltpu.make_async_copy(
            x_ref.at[:, pl.ds(j * width, width)], own.at[j, pl.ds(0, users)], load_sem.at[j]
        )
        for j in range(CHUNKS)
    ]
    for load in loads:
        load.start()

    barrier = pltpu.get_barrier_semaphore()

    def greet(device):
        pl.semaphore_signal(barrier, inc=1, device_id=device, device_id_type=MESH)

    for device in (right, left, mate, twin):
        greet(device)

    @pl.when(seconds)
    def _():
        greet(after[0])
        greet(after[1])

    @pl.when(seconds & (y == 3))
    def _():
        greet(relay_from[0])
        greet(relay_from[1])
        greet(relay_after)

    own[:, pl.ds(users, PADDED - users), :] = jnp.zeros(
        (CHUNKS, PADDED - users, width), own.dtype
    )
    partner[:, pl.ds(users, PADDED - users), :] = jnp.zeros(
        (units, PADDED - users, width), partner.dtype
    )
    relays = jnp.where((y == 0) | (seconds & (y == 3)), 1, 0)
    pl.semaphore_wait(barrier, 5 + relays)

    def send(source, target, sent, landed, device):
        return pltpu.make_async_remote_copy(
            src_ref=source,
            dst_ref=target,
            send_sem=sent,
            recv_sem=landed,
            device_id=device,
            device_id_type=MESH,
        )

    def block(ref, at):
        return ref.at[at, pl.ds(0, users)]

    def pass_on(j, unit, sent):
        def direct():
            send(block(own, j), block(partner, unit), sent, block_recv.at[unit], before).start()

        if j in RELAYED:
            slot = unit // CHUNKS * len(RELAYED) + RELAYED.index(j)

            @pl.when(y == 0)
            def _():
                send(block(own, j), relay.at[slot], sent, relay_recv.at[slot], relay_at).start()

            @pl.when(y != 0)
            def _():
                direct()
        else:
            direct()

    def relay_on(slot):
        unit = slot // len(RELAYED) * CHUNKS + RELAYED[slot % len(RELAYED)]
        copy = send(
            relay.at[slot],
            block(partner, unit),
            block_send.at[12 + slot],
            block_recv.at[unit],
            relay_to,
        )
        send(
            relay.at[slot], relay.at[slot], block_send.at[12 + slot], relay_recv.at[slot], relay_to
        ).wait_recv()
        copy.start()

    for j in range(CHUNKS):
        loads[j].wait()

        @pl.when(core == 0)
        def _():
            pass_on(j, j, block_send.at[j])

        @pl.when(seconds)
        def _():
            send(
                block(own, j), block(partner, j), block_send.at[j], block_recv.at[j], twin
            ).start()

    def weigh(step):
        values = own[lax.rem(x + step, RING)].astype(jnp.float32)
        weighted[step] = (values.T * weight_ref[0:1, :] * weight_ref[1:2, :]).astype(
            weighted.dtype
        )

    def gram(step, unit, start, count):
        return jnp.dot(
            weighted[step, pl.ds(start, count)],
            partner[unit],
            preferred_element_type=jnp.float32,
        )

    weigh(2)

    @pl.when(seconds & (y == 3))
    def _():
        relay_on(0)

    def first_copy(unit, way):
        return send(
            first_out.at[unit, way],
            first_in.at[unit, way],
            first_send.at[way, unit],
            first_recv.at[way, unit],
            (right, left)[way],
        )

    def second_copy(unit, way):
        return send(
            second_out.at[unit, way],
            second_in.at[unit, way],
            second_send.at[way, unit],
            second_recv.at[way, unit],
            (right, left)[way],
        )

    def pair_copy(unit):
        return send(
            pair_out.at[unit], pair_in.at[unit], pair_send.at[unit], pair_recv.at[unit], mate
        )

    def store(unit):
        column = pl.multiple_of(lax.rem(unit, CHUNKS) * width, width)
        return pltpu.make_async_copy(
            total.at[unit],
            out_ref.at[unit // CHUNKS, :, pl.ds(column, width)],
            store_sem.at[unit],
        )

    def forward(unit):
        return send(
            block(partner, unit),
            block(partner, unit + CHUNKS),
            block_send.at[8 + unit],
            block_recv.at[unit + CHUNKS],
            twin,
        )

    def step(t, carry):
        @pl.when(t < units)
        def _():
            unit = t
            send(
                block(partner, unit),
                block(partner, unit),
                block_send.at[0],
                block_recv.at[unit],
                twin,
            ).wait_recv()

            @pl.when(seconds & (t < CHUNKS))
            def _():
                forward(unit).start()

            for part in range(2):
                first_out[unit, part] = gram(2, unit, part * half, half).astype(first_out.dtype)
                first_copy(unit, part).start()

            @pl.when(t == 0)
            def _():
                weigh(1)
                weigh(3)
                weigh(0)

            @pl.when(seconds & (y == 3))
            def _():
                for slot, at in ((1, 0), (2, 2), (3, 3)):

                    @pl.when(t == at)
                    def _():
                        relay_on(slot)

            for j in range(CHUNKS):

                @pl.when(seconds & (t == 1 + j // 2))
                def _():
                    pass_on(j, CHUNKS + j, block_send.at[CHUNKS + j])

        @pl.when((t >= 1) & (t < units + 1))
        def _():
            unit = t - 1
            for way in range(2):
                toward = (1, 3)[way]
                first_copy(unit, way).wait_recv()
                merged = gram(toward, unit, way * half, half) + first_in[unit, way].astype(
                    jnp.float32
                )
                second_out[unit, way, way] = merged.astype(second_out.dtype)
                second_out[unit, way, 1 - way] = gram(
                    toward, unit, (1 - way) * half, half
                ).astype(second_out.dtype)
                second_copy(unit, way).start()

        @pl.when((t >= 2) & (t < units + 2))
        def _():
            unit = t - 2
            for way in range(2):
                second_copy(unit, way).wait_recv()

            def gathered(part):
                start = pl.multiple_of(part * half, half)
                return (
                    gram(0, unit, start, half)
                    + second_in[unit, 0, part].astype(jnp.float32)
                    + second_in[unit, 1, part].astype(jnp.float32)
                )

            pair_out[unit] = gathered(1 - z_lo).astype(pair_out.dtype)
            pair_copy(unit).start()
            total[unit] = gathered(z_lo)

        @pl.when(t >= 3)
        def _():
            unit = t - 3
            pair_copy(unit).wait_recv()
            total[unit] = total[unit] + pair_in[unit].astype(jnp.float32)
            store(unit).start()

        return carry

    lax.fori_loop(0, units + 3, step, 0)

    def finish(unit, carry):
        for way in range(2):
            first_copy(unit, way).wait_send()
            second_copy(unit, way).wait_send()
        pair_copy(unit).wait_send()
        store(unit).wait()
        return carry

    lax.fori_loop(0, units, finish, 0)

    def sent(at):
        send(
            block(own, 0), block(partner, 0), block_send.at[at], block_recv.at[0], twin
        ).wait_send()

    for j in range(CHUNKS):
        sent(j)

        @pl.when(seconds)
        def _():
            sent(CHUNKS + j)
            sent(2 * CHUNKS + j)

    @pl.when(seconds & (y == 3))
    def _():
        for slot in range(2 * len(RELAYED)):
            sent(12 + slot)


def on_device(interactions, user_weight):
    users, items = interactions.shape
    slabs = lax.axis_size("slab")
    scale = 1.0 / jnp.sqrt(jnp.float32(users * slabs))
    weights = jnp.stack(
        [jnp.pad(user_weight, (0, PADDED - users)), jnp.full((PADDED,), scale, jnp.float32)]
    )
    width, rows = items // CHUNKS, items // RING
    half = rows // 2
    units = ROUNDS * CHUNKS
    half_type = interactions.dtype
    dma = pltpu.SemaphoreType.DMA
    return pl.pallas_call(
        kernel,
        name="gram_tiles",
        out_shape=jax.ShapeDtypeStruct((ROUNDS, items // slabs, items), jnp.float32),
        in_specs=[
            pl.BlockSpec(memory_space=pl.ANY),
            pl.BlockSpec(memory_space=pltpu.VMEM),
        ],
        out_specs=pl.BlockSpec(memory_space=pl.ANY),
        scratch_shapes=[
            pltpu.VMEM((CHUNKS, PADDED, width), half_type),
            pltpu.VMEM((RING, rows, PADDED), half_type),
            pltpu.VMEM((units, PADDED, width), half_type),
            pltpu.VMEM((ROUNDS * len(RELAYED), users, width), half_type),
            pltpu.VMEM((units, 2, half, width), half_type),
            pltpu.VMEM((units, 2, half, width), half_type),
            pltpu.VMEM((units, 2, 2, half, width), half_type),
            pltpu.VMEM((units, 2, 2, half, width), half_type),
            pltpu.VMEM((units, half, width), half_type),
            pltpu.VMEM((units, half, width), half_type),
            pltpu.VMEM((units, half, width), jnp.float32),
            dma((CHUNKS,)),
            dma((16,)),
            dma((units,)),
            dma((ROUNDS * len(RELAYED),)),
            dma((2, units)),
            dma((2, units)),
            dma((2, units)),
            dma((2, units)),
            dma((units,)),
            dma((units,)),
            dma((units,)),
        ],
        compiler_params=pltpu.CompilerParams(
            collective_id=0, has_side_effects=True, vmem_limit_bytes=60 << 20
        ),
        cost_estimate=pl.CostEstimate(
            flops=ROUNDS * 2 * items * items * users,
            bytes_accessed=users * items * 2 + ROUNDS * items // slabs * items * 4,
            transcendentals=0,
        ),
    )(interactions, weights)


def solution(mesh):
    in_specs = (P("slab", "blk"), P("slab"))
    out_specs = P(None, ("blk", "slab"), None)
    return jax.shard_map(
        on_device, mesh=mesh, in_specs=in_specs, out_specs=out_specs, check_vma=False
    )
```

time: 532 us -> 187 us (0.35)
  the two profiles are of different devices: /device:TPU:1 before, /device:TPU:249 now
where the time goes in v1:
time: 187 us
  Pallas kernels  181 us (97%)
  local copies, waits for them, and re-layouts  6 us (3%)
    pallas_call x1, Pallas kernels, on_device(): pl.pallas_call(kernel, name='gram_tiles', out_shape=jax.ShapeDtypeStruct(...  181 us
    unnamed x1, local copies, waits for them, and re-layouts  4.7 us

profile of v1, /device:TPU:249, one launch (start us, length us, event | category | flops | bytes accessed | tf_op | source)
XLA Modules:
  0.0 187.2 jit_solution(9114531839896073060)
XLA Ops:
  0.0 0.7 pad.5
  0.7 0.6 stack.7.weight_ref
  1.3 181.2 %gram_tiles.1 = f32[2,256,2048]{2,1,0:T(8,128)} custom-call(bf16[880,2048]{1,0:T(8,128)(2,1)} %x_ref.1, f32[2,896]{1,0:T(2,128)} %stack.7.weight_ref), custom_call_target="tpu_custom_call" | custom-call | flops 14763950080 | bytes 7798784 | tf_op jit(solution)/shard_map/gram_tiles/pallas_call | solution.py:347
  182.5 4.7 %copy.4 = f32[2,256,2048]{2,1,0:T(8,128)} copy(f32[2,256,2048]{2,1,0:T(8,128)} %gram_tiles.1) | data formatting | bytes 8388608
  (1 shorter events, 0.0 us)

commit v2 on v1

v2 whole, which is shorter than its diff:
```python
import functools

import jax
import jax.numpy as jnp
from jax import lax
from jax.experimental import pallas as pl
from jax.experimental.pallas import tpu as pltpu
from jax.sharding import PartitionSpec as P

ROUNDS = 2
CHUNKS = 8
RING = 4
PADDED = 896
PAIR_FIRST = (((), ()), ((5, 7, 9, 11), (4, 6, 8, 10, 12)))
EARLY = max(len(of) for halves in PAIR_FIRST for of in halves)
LAG = 4
STAGES = (1, 3, 5)
ITERATIONS = max([ROUNDS * CHUNKS + STAGES[2]] + [u + LAG + STAGES[1] + 1 for halves in PAIR_FIRST for of in halves for u in of])
PASS_AT = (3, 3, 3, 4, 5, 5, 5, 6)
RELAY_AT = {1: (0, 2, 6, 10), 2: (1, 3, 6, 10), 3: (-1, 1, 6, 10)}
MESH = pl.DeviceIdType.MESH


def kernel(
    x_ref,
    weight_ref,
    out_ref,
    own,
    weighted,
    partner,
    relay,
    first_out,
    first_in,
    second_out,
    second_in,
    pair_out,
    pair_in,
    early_out,
    early_in,
    total,
    load_sem,
    block_send,
    block_recv,
    relay_recv,
    first_send,
    first_recv,
    second_send,
    second_recv,
    pair_send,
    pair_recv,
    early_send,
    early_recv,
    store_sem,
):
    blk, slab = lax.axis_index("blk"), lax.axis_index("slab")
    blocks = lax.axis_size("blk")
    core, y = lax.rem(blk, 2), lax.rem(blk // 2, 4)
    x, z_lo = slab // 2, lax.rem(slab, 2)
    users = x_ref.shape[0]
    width = x_ref.shape[1] // CHUNKS
    rows = x_ref.shape[1] // RING
    half = rows // 2
    quarter = half // 2
    units = ROUNDS * CHUNKS
    seconds = core == 1

    right = (blk, lax.rem(x + 1, RING) * 2 + z_lo)
    left = (blk, lax.rem(x + RING - 1, RING) * 2 + z_lo)
    mate = (blk, x * 2 + 1 - z_lo)
    twin = (blk + 1 - 2 * core, slab)
    back = lax.rem(blk + blocks - 2 - core, blocks) + 1
    before = (back, slab)
    front = lax.rem(blk - core + 2, blocks)
    after = ((front, slab), (front + 1, slab))
    base = blk - lax.rem(blk, 8)
    relay_at = [(base + 2 * at + 1 - core, slab) for at in (3, 1, 2)]
    relay_from = (base + 1 - core, slab)
    relay_to = (lax.rem(base + blocks - 8, blocks) + 7, slab)
    relay_after = [(lax.rem(base + 8, blocks) + at, slab) for at in range(2, 8)]

    loads = [
        pltpu.make_async_copy(
            x_ref.at[:, pl.ds(j * width, width)], own.at[j, pl.ds(0, users)], load_sem.at[j]
        )
        for j in range(CHUNKS)
    ]
    for load in loads:
        load.start()

    barrier = pltpu.get_barrier_semaphore()

    def greet(device):
        pl.semaphore_signal(barrier, inc=1, device_id=device, device_id_type=MESH)

    for device in (right, left, mate, twin):
        greet(device)

    @pl.when(seconds)
    def _():
        greet(after[0])
        greet(after[1])

    @pl.when(y != 0)
    def _():
        greet(relay_from)

    @pl.when(seconds & (y == 3))
    def _():
        for device in relay_after:
            greet(device)

    own[:, pl.ds(users, PADDED - users), :] = jnp.zeros(
        (CHUNKS, PADDED - users, width), own.dtype
    )
    early_in[early_in.shape[0] - 1] = jnp.zeros((half, width), early_in.dtype)
    partner[:, pl.ds(users, PADDED - users), :] = jnp.zeros(
        (units, PADDED - users, width), partner.dtype
    )
    relays = jnp.where(y == 0, 3, 1)
    pl.semaphore_wait(barrier, 5 + relays)

    def send(source, target, sent, landed, device):
        return pltpu.make_async_remote_copy(
            src_ref=source,
            dst_ref=target,
            send_sem=sent,
            recv_sem=landed,
            device_id=device,
            device_id_type=MESH,
        )

    def block(ref, at):
        return ref.at[at, pl.ds(0, users)]

    def pass_on(j, unit, sent):
        def direct():
            send(block(own, j), block(partner, unit), sent, block_recv.at[unit], before).start()

        if j % 4 == 0:
            direct()
        else:
            slot = unit // 4

            @pl.when(y == 0)
            def _():
                send(
                    block(own, j), relay.at[slot], sent, relay_recv.at[slot], relay_at[j % 4 - 1]
                ).start()

            @pl.when(y != 0)
            def _():
                direct()

    def relay_on(slot):
        unit = slot * 4 + lax.rem(y, 3) + 1
        sent = block_send.at[3 * CHUNKS + slot]
        send(relay.at[slot], relay.at[slot], sent, relay_recv.at[slot], relay_to).wait_recv()
        send(relay.at[slot], block(partner, unit), sent, block_recv.at[unit], relay_to).start()

    for j in range(CHUNKS):
        loads[j].wait()

        @pl.when(core == 0)
        def _():
            pass_on(j, j, block_send.at[j])

        @pl.when(seconds)
        def _():
            send(
                block(own, j), block(partner, j), block_send.at[j], block_recv.at[j], twin
            ).start()

    def weigh(step):
        for piece in range(rows // width):
            values = own[lax.rem(x + step, RING) * (rows // width) + piece].T.astype(jnp.float32)
            weighted[step, pl.ds(piece * width, width)] = (
                values * weight_ref[0:1, :] * weight_ref[1:2, :]
            ).astype(weighted.dtype)

    def weigh_rest():
        for step in (1, 3, 0):
            weigh(step)

    def gram(step, unit, part):
        start = pl.multiple_of(part * half, half)
        return jnp.dot(
            weighted[step, pl.ds(start, half)],
            partner[unit],
            preferred_element_type=jnp.float32,
        )

    weigh(2)

    @pl.when(seconds)
    def _():
        weigh_rest()

    def pair_first(unit, part):
        def among(of):
            return functools.reduce(jnp.logical_or, [unit == u for u in of], unit < 0)

        at = [[among(of) for of in halves] for halves in PAIR_FIRST]
        return jnp.where(
            core == 0,
            jnp.where(part == 0, at[0][0], at[0][1]),
            jnp.where(part == 0, at[1][0], at[1][1]),
        )

    def relay_steps(t):
        for slot in range(units // 4):
            at = jnp.where(y == 1, RELAY_AT[1][slot], jnp.where(y == 2, RELAY_AT[2][slot], RELAY_AT[3][slot]))

            @pl.when((core == 1 - slot // (CHUNKS // 4)) & (y != 0) & (t == at))
            def _():
                relay_on(slot)

    def first_copy(job, way):
        return send(
            first_out.at[job, way],
            first_in.at[job, way],
            first_send.at[way, job],
            first_recv.at[way, job],
            (right, left)[way],
        )

    def second_copy(job, way):
        return send(
            second_out.at[job, way],
            second_in.at[job, way],
            second_send.at[way, job],
            second_recv.at[way, job],
            (right, left)[way],
        )

    def pair_copy(unit):
        return send(
            pair_out.at[unit], pair_in.at[unit], pair_send.at[unit], pair_recv.at[unit], mate
        )

    def early_copy(at):
        return send(
            early_out.at[at], early_in.at[at], early_send.at[at], early_recv.at[at], mate
        )

    def early_at(unit, step, part):
        before = [[sum([jnp.where(unit > u, 1, 0) for u in of]) for of in halves] for halves in PAIR_FIRST]
        at = jnp.where(
            core == 0,
            jnp.where(part == 0, before[0][0], before[0][1]),
            jnp.where(part == 0, before[1][0], before[1][1]),
        )
        return at * RING + step

    def store(unit):
        column = pl.multiple_of(lax.rem(unit, CHUNKS) * width, width)
        return pltpu.make_async_copy(
            total.at[unit],
            out_ref.at[unit // CHUNKS, :, pl.ds(column, width)],
            store_sem.at[unit],
        )

    def forward(unit):
        return send(
            block(partner, unit),
            block(partner, unit + CHUNKS),
            block_send.at[2 * CHUNKS + unit],
            block_recv.at[unit + CHUNKS],
            twin,
        )

    def job_of(kind, stage):
        late = kind == 2
        unit = stage - jnp.where(late, LAG, 0)
        mine = jnp.where(kind > 0, 1, 0)
        part = jnp.where(kind > 0, z_lo, 1 - z_lo)
        active = (unit >= 0) & (unit < units) & (pair_first(unit, part) == late)
        return late, unit, mine, part, active

    def each_kind(stage, work):
        def one(kind, carry):
            late, unit, mine, part, active = job_of(kind, stage)

            @pl.when(active)
            def _():
                work(late, unit, mine, part, unit * 2 + mine)

            return carry

        lax.fori_loop(0, 3, one, 0)

    def paired(late, unit, step, part):
        at = jnp.where(late, early_at(unit, step, part), early_in.shape[0] - 1)

        @pl.when(late)
        def _():
            early_copy(at).wait_recv()

        return gram(step, unit, part) + early_in[at].astype(jnp.float32)

    def first_step(late, unit, mine, part, job):
        value = paired(late, unit, 2, part).astype(first_out.dtype)
        for way in range(2):
            first_out[job, way] = value[way * quarter : (way + 1) * quarter]
            first_copy(job, way).start()

    def second_step(late, unit, mine, part, job):
        for way in range(2):
            value = paired(late, unit, (1, 3)[way], part)
            first_copy(job, way).wait_recv()
            joined = slice(way * quarter, (way + 1) * quarter)
            plain = slice((1 - way) * quarter, (2 - way) * quarter)
            second_out[job, way, joined] = (
                value[joined] + first_in[job, way].astype(jnp.float32)
            ).astype(second_out.dtype)
            second_out[job, way, plain] = value[plain].astype(second_out.dtype)
            second_copy(job, way).start()

    def third_step(late, unit, mine, part, job):
        value = paired(late, unit, 0, part)
        for way in range(2):
            second_copy(job, way).wait_recv()
        value = (
            value
            + second_in[job, 0].astype(jnp.float32)
            + second_in[job, 1].astype(jnp.float32)
        )

        @pl.when(mine == 0)
        def _():
            pair_out[unit] = value.astype(pair_out.dtype)
            pair_copy(unit).start()

        @pl.when(mine == 1)
        def _():
            total[unit] = value

        @pl.when(late)
        def _():
            store(unit).start()

    def last_step(unit):
        pair_copy(unit).wait_recv()
        total[unit] = total[unit] + pair_in[unit].astype(jnp.float32)
        store(unit).start()

    def step(t, carry):
        @pl.when(t < units)
        def _():
            send(
                block(partner, t), block(partner, t), block_send.at[0], block_recv.at[t], twin
            ).wait_recv()

            @pl.when(seconds & (t < CHUNKS))
            def _():
                forward(t).start()

            @pl.when(pair_first(t, 1 - z_lo))
            def _():
                def early(i, carry):
                    toward = lax.rem(i + 2, RING)
                    at = early_at(t, toward, 1 - z_lo)
                    early_out[at] = gram(toward, t, 1 - z_lo).astype(early_out.dtype)
                    early_copy(at).start()
                    return carry

                lax.fori_loop(0, RING, early, 0)

        each_kind(t, first_step)

        @pl.when((core == 0) & (t == 0))
        def _():
            weigh_rest()

        for j in range(CHUNKS):

            @pl.when(seconds & (t == PASS_AT[j]))
            def _():
                pass_on(j, CHUNKS + j, block_send.at[CHUNKS + j])

        relay_steps(t)
        each_kind(t - STAGES[0], second_step)
        each_kind(t - STAGES[1], third_step)
        unit = t - STAGES[2]

        @pl.when((unit >= 0) & (unit < units) & jnp.logical_not(pair_first(unit, z_lo)))
        def _():
            last_step(unit)

        return carry

    relay_steps(-1)
    lax.fori_loop(0, ITERATIONS, step, 0)

    def finish(unit, carry):
        store(unit).wait()
        ahead = pair_first(unit, 1 - z_lo)

        @pl.when(ahead)
        def _():
            for toward in range(RING):
                early_copy(early_at(unit, toward, 1 - z_lo)).wait_send()

        @pl.when(jnp.logical_not(ahead))
        def _():
            pair_copy(unit).wait_send()
            for way in range(2):
                first_copy(unit * 2, way).wait_send()
                second_copy(unit * 2, way).wait_send()

        for way in range(2):
            first_copy(unit * 2 + 1, way).wait_send()
            second_copy(unit * 2 + 1, way).wait_send()
        return carry

    lax.fori_loop(0, units, finish, 0)

    def sent(at):
        send(
            block(own, 0), block(partner, 0), block_send.at[at], block_recv.at[0], twin
        ).wait_send()

    for j in range(CHUNKS):
        sent(j)

        @pl.when(seconds)
        def _():
            sent(CHUNKS + j)
            sent(2 * CHUNKS + j)

    for slot in range(units // 4):

        @pl.when((core == 1 - slot // (CHUNKS // 4)) & (y != 0))
        def _():
            sent(3 * CHUNKS + slot)


def on_device(interactions, user_weight):
    users, items = interactions.shape
    slabs = lax.axis_size("slab")
    scale = 1.0 / jnp.sqrt(jnp.float32(users * slabs))
    weights = jnp.stack(
        [jnp.pad(user_weight, (0, PADDED - users)), jnp.full((PADDED,), scale, jnp.float32)]
    )
    width, rows = items // CHUNKS, items // RING
    half = rows // 2
    units = ROUNDS * CHUNKS
    jobs, early = 2 * units, EARLY * RING
    half_type = interactions.dtype
    dma = pltpu.SemaphoreType.DMA
    return pl.pallas_call(
        kernel,
        name="gram_tiles",
        out_shape=jax.ShapeDtypeStruct((ROUNDS, items // slabs, items), jnp.float32),
        in_specs=[
            pl.BlockSpec(memory_space=pl.ANY),
            pl.BlockSpec(memory_space=pltpu.VMEM),
        ],
        out_specs=pl.BlockSpec(memory_space=pl.ANY),
        scratch_shapes=[
            pltpu.VMEM((CHUNKS, PADDED, width), half_type),
            pltpu.VMEM((RING, rows, PADDED), half_type),
            pltpu.VMEM((units, PADDED, width), half_type),
            pltpu.VMEM((units // 4, users, width), half_type),
            pltpu.VMEM((jobs, 2, half // 2, width), half_type),
            pltpu.VMEM((jobs, 2, half // 2, width), half_type),
            pltpu.VMEM((jobs, 2, half, width), half_type),
            pltpu.VMEM((jobs, 2, half, width), half_type),
            pltpu.VMEM((units, half, width), half_type),
            pltpu.VMEM((units, half, width), half_type),
            pltpu.VMEM((early, half, width), half_type),
            pltpu.VMEM((early + 1, half, width), half_type),
            pltpu.VMEM((units, half, width), jnp.float32),
            dma((CHUNKS,)),
            dma((3 * CHUNKS + units // 4,)),
            dma((units,)),
            dma((units // 4,)),
            dma((2, jobs)),
            dma((2, jobs)),
            dma((2, jobs)),
            dma((2, jobs)),
            dma((units,)),
            dma((units,)),
            dma((early,)),
            dma((early,)),
            dma((units,)),
        ],
        compiler_params=pltpu.CompilerParams(
            collective_id=0, has_side_effects=True, vmem_limit_bytes=62 << 20
        ),
        cost_estimate=pl.CostEstimate(
            flops=ROUNDS * 2 * items * items * users,
            bytes_accessed=users * items * 2 + ROUNDS * items // slabs * items * 4,
            transcendentals=0,
        ),
    )(interactions, weights)


def solution(mesh):
    in_specs = (P("slab", "blk"), P("slab"))
    out_specs = P(None, ("blk", "slab"), None)
    return jax.shard_map(
        on_device, mesh=mesh, in_specs=in_specs, out_specs=out_specs, check_vma=False
    )
```

time: 187 us -> 157 us (0.84)
  the two profiles are of different devices: /device:TPU:249 before, /device:TPU:1 now
where the time goes in v2:
time: 157 us; the launch traced here: 155 us
  Pallas kernels  149 us (95%)
  local copies, waits for them, and re-layouts  6 us (4%)
    pallas_call x1, Pallas kernels, on_device(): pl.pallas_call(kernel, name='gram_tiles', out_shape=jax.ShapeDtypeStruct(...  149 us
    unnamed x1, local copies, waits for them, and re-layouts  4.7 us

profile of v2, /device:TPU:1, one launch (start us, length us, event | category | flops | bytes accessed | tf_op | source)
XLA Modules:
  0.0 155.0 jit_solution(674092017174241466)
XLA Ops:
  0.0 0.7 pad.5
  0.7 0.6 stack.7.weight_ref
  1.3 149.0 %gram_tiles.1 = f32[2,256,2048]{2,1,0:T(8,128)} custom-call(bf16[880,2048]{1,0:T(8,128)(2,1)} %x_ref.1, f32[2,896]{1,0:T(2,128)} %stack.7.weight_ref), custom_call_target="tpu_custom_call" | custom-call | flops 14763950080 | bytes 7798784 | tf_op jit(solution)/shard_map/gram_tiles/pallas_call | solution.py:450
  150.3 4.7 %copy.4 = f32[2,256,2048]{2,1,0:T(8,128)} copy(f32[2,256,2048]{2,1,0:T(8,128)} %gram_tiles.1) | data formatting | bytes 8388608
  (1 shorter events, 0.0 us)

commit v3 on v2

--- a/solution.py
+++ b/solution.py
@@ -2,6 +2,7 @@
 
 import jax
 import jax.numpy as jnp
+import numpy as np
 from jax import lax
 from jax.experimental import pallas as pl
 from jax.experimental.pallas import tpu as pltpu
@@ -17,7 +18,8 @@
 STAGES = (1, 3, 5)
 ITERATIONS = max([ROUNDS * CHUNKS + STAGES[2]] + [u + LAG + STAGES[1] + 1 for halves in PAIR_FIRST for of in halves for u in of])
 PASS_AT = (3, 3, 3, 4, 5, 5, 5, 6)
-RELAY_AT = {1: (0, 2, 6, 10), 2: (1, 3, 6, 10), 3: (-1, 1, 6, 10)}
+WRAP_AT = (3, 3, 3, 4, 5, 5, 5, 6)
+RELAY_AT = {1: (0, 2, 9, 13), 2: (1, 3, 9, 13), 3: (-1, 1, 7, 11)}
 MESH = pl.DeviceIdType.MESH
 
 
@@ -25,6 +27,7 @@
     x_ref,
     weight_ref,
     out_ref,
+    padded_weight,
     own,
     weighted,
     partner,
@@ -61,6 +64,7 @@
     rows = x_ref.shape[1] // RING
     half = rows // 2
     quarter = half // 2
+    scale = np.float32(1) / np.sqrt(np.float32(users * lax.axis_size("slab")))
     units = ROUNDS * CHUNKS
     seconds = core == 1
 
@@ -109,6 +113,8 @@
         for device in relay_after:
             greet(device)
 
+    padded_weight[...] = jnp.zeros(padded_weight.shape, padded_weight.dtype)
+    padded_weight[:, pl.ds(0, users)] = weight_ref[...]
     own[:, pl.ds(users, PADDED - users), :] = jnp.zeros(
         (CHUNKS, PADDED - users, width), own.dtype
     )
@@ -174,7 +180,7 @@
         for piece in range(rows // width):
             values = own[lax.rem(x + step, RING) * (rows // width) + piece].T.astype(jnp.float32)
             weighted[step, pl.ds(piece * width, width)] = (
-                values * weight_ref[0:1, :] * weight_ref[1:2, :]
+                values * padded_weight[...] * scale
             ).astype(weighted.dtype)
 
     def weigh_rest():
@@ -254,7 +260,7 @@
     def store(unit):
         column = pl.multiple_of(lax.rem(unit, CHUNKS) * width, width)
         return pltpu.make_async_copy(
-            total.at[unit],
+            pair_in.at[unit],
             out_ref.at[unit // CHUNKS, :, pl.ds(column, width)],
             store_sem.at[unit],
         )
@@ -330,17 +336,18 @@
             pair_out[unit] = value.astype(pair_out.dtype)
             pair_copy(unit).start()
 
-        @pl.when(mine == 1)
+        @pl.when((mine == 1) & jnp.logical_not(late))
         def _():
             total[unit] = value
 
         @pl.when(late)
         def _():
+            pair_in[unit] = value.astype(pair_in.dtype)
             store(unit).start()
 
     def last_step(unit):
         pair_copy(unit).wait_recv()
-        total[unit] = total[unit] + pair_in[unit].astype(jnp.float32)
+        pair_in[unit] = (total[unit] + pair_in[unit].astype(jnp.float32)).astype(pair_in.dtype)
         store(unit).start()
 
     def step(t, carry):
@@ -373,7 +380,7 @@
 
         for j in range(CHUNKS):
 
-            @pl.when(seconds & (t == PASS_AT[j]))
+            @pl.when(seconds & (t == jnp.where(y == 0, WRAP_AT[j], PASS_AT[j])))
             def _():
                 pass_on(j, CHUNKS + j, block_send.at[CHUNKS + j])
 
@@ -437,26 +444,23 @@
 def on_device(interactions, user_weight):
     users, items = interactions.shape
     slabs = lax.axis_size("slab")
-    scale = 1.0 / jnp.sqrt(jnp.float32(users * slabs))
-    weights = jnp.stack(
-        [jnp.pad(user_weight, (0, PADDED - users)), jnp.full((PADDED,), scale, jnp.float32)]
-    )
     width, rows = items // CHUNKS, items // RING
     half = rows // 2
     units = ROUNDS * CHUNKS
     jobs, early = 2 * units, EARLY * RING
     half_type = interactions.dtype
     dma = pltpu.SemaphoreType.DMA
-    return pl.pallas_call(
+    tiles = pl.pallas_call(
         kernel,
         name="gram_tiles",
-        out_shape=jax.ShapeDtypeStruct((ROUNDS, items // slabs, items), jnp.float32),
+        out_shape=jax.ShapeDtypeStruct((ROUNDS, items // slabs, items), half_type),
         in_specs=[
             pl.BlockSpec(memory_space=pl.ANY),
             pl.BlockSpec(memory_space=pltpu.VMEM),
         ],
         out_specs=pl.BlockSpec(memory_space=pl.ANY),
         scratch_shapes=[
+            pltpu.VMEM((1, PADDED), jnp.float32),
             pltpu.VMEM((CHUNKS, PADDED, width), half_type),
             pltpu.VMEM((RING, rows, PADDED), half_type),
             pltpu.VMEM((units, PADDED, width), half_type),
@@ -489,10 +493,11 @@
         ),
         cost_estimate=pl.CostEstimate(
             flops=ROUNDS * 2 * items * items * users,
-            bytes_accessed=users * items * 2 + ROUNDS * items // slabs * items * 4,
+            bytes_accessed=users * items * 2 + ROUNDS * items // slabs * items * 2,
             transcendentals=0,
         ),
-    )(interactions, weights)
+    )(interactions, user_weight.reshape(1, users))
+    return tiles.astype(jnp.float32)
 
 
 def solution(mesh):

time: 157 us -> 154 us (0.981); the launches traced: 155 us -> 154 us
  local copies, waits for them, and re-layouts: 6 us -> 1.27 us
  other arithmetic: 0 us -> 4.13 us
    unnamed x1 -> x0, local copies, waits for them, and re-layouts: 4.7 us -> none
    convert_element_type x0 -> x1, other arithmetic: none -> 4.13 us  [on_device(): return tiles.astype(jnp.float32)]
where the time goes in v3:
time: 154 us
  Pallas kernels  148 us (96%)
  other arithmetic  4.13 us (3%)
    pallas_call x1, Pallas kernels, on_device(): pl.pallas_call(kernel, name='gram_tiles', out_shape=jax.ShapeDtypeStruct(...  148 us
    convert_element_type x1, other arithmetic, on_device(): return tiles.astype(jnp.float32)  4.13 us

profile of v3, /device:TPU:1, one launch (start us, length us, event | category | flops | bytes accessed | tf_op | source)
XLA Modules:
  0.0 153.6 jit_solution(232059356299356911)
XLA Ops:
  0.0 1.3 reshape.3.weight_ref
  1.3 148.2 %gram_tiles.1 = bf16[2,256,2048]{2,1,0:T(8,128)(2,1)} custom-call(bf16[880,2048]{1,0:T(8,128)(2,1)} %x_ref.1, f32[1,880]{1,0:T(1,128)} %reshape.3.weight_ref), custom_call_target="tpu_custom_call" | custom-call | flops 14763950080 | bytes 5701632 | tf_op jit(solution)/shard_map/gram_tiles/pallas_call | solution.py:453
  149.4 4.1 %convert_element_type.3 = f32[2,256,2048]{2,1,0:T(8,128)} convert(bf16[2,256,2048]{2,1,0:T(8,128)(2,1)} %gram_tiles.1) | non-fusion elementwise | flops 1048576 | bytes 6291456 | tf_op jit(solution)/shard_map/convert_element_type | solution.py:500

commit v4 on v3

--- a/solution.py
+++ b/solution.py
@@ -12,14 +12,15 @@
 CHUNKS = 8
 RING = 4
 PADDED = 896
-PAIR_FIRST = (((), ()), ((5, 7, 9, 11), (4, 6, 8, 10, 12)))
-EARLY = max(len(of) for halves in PAIR_FIRST for of in halves)
-LAG = 4
-STAGES = (1, 3, 5)
-ITERATIONS = max([ROUNDS * CHUNKS + STAGES[2]] + [u + LAG + STAGES[1] + 1 for halves in PAIR_FIRST for of in halves for u in of])
+PAIR_FIRST = ((((10, 12), (10, 12)), ((5, 7, 9, 11), (4, 6, 8, 10, 12))), (((), ()), ((5, 7, 9, 11), (4, 6, 8, 10, 12))))
+EARLY = max(len(of) for cores in PAIR_FIRST for halves in cores for of in halves)
+LAG = 6
+STAGES = (1, 3, 8)
+ITERATIONS = max([ROUNDS * CHUNKS + STAGES[2]] + [u + LAG + STAGES[1] + 1 for cores in PAIR_FIRST for halves in cores for of in halves for u in of])
 PASS_AT = (3, 3, 3, 4, 5, 5, 5, 6)
-WRAP_AT = (3, 3, 3, 4, 5, 5, 5, 6)
-RELAY_AT = {1: (0, 2, 9, 13), 2: (1, 3, 9, 13), 3: (-1, 1, 7, 11)}
+WRAP_AT = (3, 2, 2, 3, 4, 3, 4, 4)
+RELAY_AT = {1: (1, 3, 7, 10), 2: (0, 2, 8, 11), 3: (-1, 1, 6, 9)}
+AGAIN_AT = (3, 5, 9, 12)
 MESH = pl.DeviceIdType.MESH
 
 
@@ -32,6 +33,7 @@
     weighted,
     partner,
     relay,
+    relay2,
     first_out,
     first_in,
     second_out,
@@ -45,6 +47,7 @@
     block_send,
     block_recv,
     relay_recv,
+    relay2_recv,
     first_send,
     first_recv,
     second_send,
@@ -77,10 +80,13 @@
     front = lax.rem(blk - core + 2, blocks)
     after = ((front, slab), (front + 1, slab))
     base = blk - lax.rem(blk, 8)
-    relay_at = [(base + 2 * at + 1 - core, slab) for at in (3, 1, 2)]
+    relay_at = [(base + 2 * at + 1 - core, slab) for at in (3, 2, 1)]
     relay_from = (base + 1 - core, slab)
-    relay_to = (lax.rem(base + blocks - 8, blocks) + 7, slab)
-    relay_after = [(lax.rem(base + 8, blocks) + at, slab) for at in range(2, 8)]
+    onward = lax.rem(base + blocks - 8, blocks)
+    relay_to = (onward + jnp.where(y == 1, 4 + core, 7), slab)
+    second_to = (base + 7, slab)
+    second_from = (lax.rem(base + 8, blocks) + 2 + core, slab)
+    relay_after = [(lax.rem(base + 8, blocks) + at, slab) for at in range(4, 8)]
 
     loads = [
         pltpu.make_async_copy(
@@ -112,6 +118,12 @@
     def _():
         for device in relay_after:
             greet(device)
+        greet((base + 4, slab))
+        greet((base + 5, slab))
+
+    @pl.when(y == 2)
+    def _():
+        greet(second_from)
 
     padded_weight[...] = jnp.zeros(padded_weight.shape, padded_weight.dtype)
     padded_weight[:, pl.ds(0, users)] = weight_ref[...]
@@ -122,7 +134,7 @@
     partner[:, pl.ds(users, PADDED - users), :] = jnp.zeros(
         (units, PADDED - users, width), partner.dtype
     )
-    relays = jnp.where(y == 0, 3, 1)
+    relays = jnp.where(y == 0, 3, jnp.where(y == 2, 2, 1))
     pl.semaphore_wait(barrier, 5 + relays)
 
     def send(source, target, sent, landed, device):
@@ -158,10 +170,31 @@
                 direct()
 
     def relay_on(slot):
-        unit = slot * 4 + lax.rem(y, 3) + 1
         sent = block_send.at[3 * CHUNKS + slot]
         send(relay.at[slot], relay.at[slot], sent, relay_recv.at[slot], relay_to).wait_recv()
-        send(relay.at[slot], block(partner, unit), sent, block_recv.at[unit], relay_to).start()
+
+        @pl.when(y == 1)
+        def _():
+            send(
+                relay.at[slot], relay2.at[slot], sent, relay2_recv.at[slot], relay_to
+            ).start()
+
+        @pl.when(y != 1)
+        def _():
+            unit = slot * 4 + 4 - y
+            send(
+                relay.at[slot], block(partner, unit), sent, block_recv.at[unit], relay_to
+            ).start()
+
+    def relay_again(slot):
+        unit = slot * 4 + 3
+        sent = block_send.at[3 * CHUNKS + units // 4 + slot]
+        send(
+            relay2.at[slot], relay2.at[slot], sent, relay2_recv.at[slot], second_to
+        ).wait_recv()
+        send(
+            relay2.at[slot], block(partner, unit), sent, block_recv.at[unit], second_to
+        ).start()
 
     for j in range(CHUNKS):
         loads[j].wait()
@@ -201,16 +234,24 @@
     def _():
         weigh_rest()
 
+    def of_this(values):
+        def pick(part):
+            return jnp.where(
+                y == 3,
+                jnp.where(core == 0, values[1][0][part], values[1][1][part]),
+                jnp.where(core == 0, values[0][0][part], values[0][1][part]),
+            )
+
+        return lambda part: jnp.where(part == 0, pick(0), pick(1))
+
+    def tabulate(work):
+        return [[[work(of) for of in halves] for halves in cores] for cores in PAIR_FIRST]
+
     def pair_first(unit, part):
         def among(of):
-            return functools.reduce(jnp.logical_or, [unit == u for u in of], unit < 0)
-
-        at = [[among(of) for of in halves] for halves in PAIR_FIRST]
-        return jnp.where(
-            core == 0,
-            jnp.where(part == 0, at[0][0], at[0][1]),
-            jnp.where(part == 0, at[1][0], at[1][1]),
-        )
+            return sum([jnp.where(unit == u, 1, 0) for u in of], 0 * unit)
+
+        return of_this(tabulate(among))(part) == 1
 
     def relay_steps(t):
         for slot in range(units // 4):
@@ -219,6 +260,10 @@
             @pl.when((core == 1 - slot // (CHUNKS // 4)) & (y != 0) & (t == at))
             def _():
                 relay_on(slot)
+
+            @pl.when((core == 1 - slot // (CHUNKS // 4)) & (y == 2) & (t == AGAIN_AT[slot]))
+            def _():
+                relay_again(slot)
 
     def first_copy(job, way):
         return send(
@@ -249,13 +294,10 @@
         )
 
     def early_at(unit, step, part):
-        before = [[sum([jnp.where(unit > u, 1, 0) for u in of]) for of in halves] for halves in PAIR_FIRST]
-        at = jnp.where(
-            core == 0,
-            jnp.where(part == 0, before[0][0], before[0][1]),
-            jnp.where(part == 0, before[1][0], before[1][1]),
-        )
-        return at * RING + step
+        def rank(of):
+            return sum([jnp.where(unit > u, 1, 0) for u in of], 0 * unit)
+
+        return of_this(tabulate(rank))(part) * RING + step
 
     def store(unit):
         column = pl.multiple_of(lax.rem(unit, CHUNKS) * width, width)
@@ -439,6 +481,10 @@
         @pl.when((core == 1 - slot // (CHUNKS // 4)) & (y != 0))
         def _():
             sent(3 * CHUNKS + slot)
+
+        @pl.when((core == 1 - slot // (CHUNKS // 4)) & (y == 2))
+        def _():
+            sent(3 * CHUNKS + units // 4 + slot)
 
 
 def on_device(interactions, user_weight):
@@ -465,6 +511,7 @@
             pltpu.VMEM((RING, rows, PADDED), half_type),
             pltpu.VMEM((units, PADDED, width), half_type),
             pltpu.VMEM((units // 4, users, width), half_type),
+            pltpu.VMEM((units // 4, users, width), half_type),
             pltpu.VMEM((jobs, 2, half // 2, width), half_type),
             pltpu.VMEM((jobs, 2, half // 2, width), half_type),
             pltpu.VMEM((jobs, 2, half, width), half_type),
@@ -475,8 +522,9 @@
             pltpu.VMEM((early + 1, half, width), half_type),
             pltpu.VMEM((units, half, width), jnp.float32),
             dma((CHUNKS,)),
-            dma((3 * CHUNKS + units // 4,)),
+            dma((3 * CHUNKS + units // 2,)),
             dma((units,)),
+            dma((units // 4,)),
             dma((units // 4,)),
             dma((2, jobs)),
             dma((2, jobs)),

time: 154 us -> 152 us (0.987); the launches traced: 154 us -> 150 us
  Pallas kernels: 148 us -> 144 us
    pallas_call x1, Pallas kernels: 148 us -> 144 us  [on_device(): pl.pallas_call(kernel, name='gram_tiles', out_shape=jax.ShapeDtypeStruct(...]
where the time goes in v4:
time: 152 us; the launch traced here: 150 us
  Pallas kernels  144 us (95%)
  other arithmetic  4.13 us (3%)
    pallas_call x1, Pallas kernels, on_device(): pl.pallas_call(kernel, name='gram_tiles', out_shape=jax.ShapeDtypeStruct(...  144 us
    convert_element_type x1, other arithmetic, on_device(): return tiles.astype(jnp.float32)  4.13 us

profile of v4, /device:TPU:1, one launch (start us, length us, event | category | flops | bytes accessed | tf_op | source)
XLA Modules:
  0.0 149.8 jit_solution(6286294633618489150)
XLA Ops:
  0.0 1.3 reshape.3.weight_ref
  1.3 144.4 %gram_tiles.1 = bf16[2,256,2048]{2,1,0:T(8,128)(2,1)} custom-call(bf16[880,2048]{1,0:T(8,128)(2,1)} %x_ref.1, f32[1,880]{1,0:T(1,128)} %reshape.3.weight_ref), custom_call_target="tpu_custom_call" | custom-call | flops 14763950080 | bytes 5701632 | tf_op jit(solution)/shard_map/gram_tiles/pallas_call | solution.py:499
  145.7 4.1 %convert_element_type.3 = f32[2,256,2048]{2,1,0:T(8,128)} convert(bf16[2,256,2048]{2,1,0:T(8,128)(2,1)} %gram_tiles.1) | non-fusion elementwise | flops 1048576 | bytes 6291456 | tf_op jit(solution)/shard_map/convert_element_type | solution.py:548

commit v5 on v4

--- a/solution.py
+++ b/solution.py
@@ -17,10 +17,10 @@
 LAG = 6
 STAGES = (1, 3, 8)
 ITERATIONS = max([ROUNDS * CHUNKS + STAGES[2]] + [u + LAG + STAGES[1] + 1 for cores in PAIR_FIRST for halves in cores for of in halves for u in of])
-PASS_AT = (3, 3, 3, 4, 5, 5, 5, 6)
-WRAP_AT = (3, 2, 2, 3, 4, 3, 4, 4)
-RELAY_AT = {1: (1, 3, 7, 10), 2: (0, 2, 8, 11), 3: (-1, 1, 6, 9)}
-AGAIN_AT = (3, 5, 9, 12)
+PASS_AT = (2, 2, 3, 3, 4, 4, 5, 5)
+WRAP_AT = (3, 2, 2, 2, 3, 3, 3, 3)
+RELAY_AT = {1: (1, 3, 6, 9), 2: (0, 2, 7, 10), 3: (-1, 1, 6, 8)}
+AGAIN_AT = (3, 5, 8, 11)
 MESH = pl.DeviceIdType.MESH
 
 

time: 152 us -> 152 us (level)
  no operation moved by 1% of the time
where the time goes in v5:
time: 152 us; the launch traced here: 150 us
  Pallas kernels  145 us (95%)
  other arithmetic  4.13 us (3%)
    pallas_call x1, Pallas kernels, on_device(): pl.pallas_call(kernel, name='gram_tiles', out_shape=jax.ShapeDtypeStruct(...  145 us
    convert_element_type x1, other arithmetic, on_device(): return tiles.astype(jnp.float32)  4.13 us

profile of v5, /device:TPU:1, one launch (start us, length us, event | category | flops | bytes accessed | tf_op | source)
XLA Modules:
  0.0 150.0 jit_solution(15084746500032340584)
XLA Ops:
  0.0 1.3 reshape.3.weight_ref
  1.3 144.6 %gram_tiles.1 = bf16[2,256,2048]{2,1,0:T(8,128)(2,1)} custom-call(bf16[880,2048]{1,0:T(8,128)(2,1)} %x_ref.1, f32[1,880]{1,0:T(1,128)} %reshape.3.weight_ref), custom_call_target="tpu_custom_call" | custom-call | flops 14763950080 | bytes 5701632 | tf_op jit(solution)/shard_map/gram_tiles/pallas_call | solution.py:499
  145.9 4.1 %convert_element_type.3 = f32[2,256,2048]{2,1,0:T(8,128)} convert(bf16[2,256,2048]{2,1,0:T(8,128)(2,1)} %gram_tiles.1) | non-fusion elementwise | flops 1048576 | bytes 6291456 | tf_op jit(solution)/shard_map/convert_element_type | solution.py:548
